TPU v7x, 32 devices: a whole 2x2x4 slice. The times are simulated.
32 devices in a mesh: tm: 8 (over z, x), sx: 2 (over core), sy: 2 (over y).
Axes of the slice: x: 2, y: 2, z: 4, core: 2. Of those that a mesh axis runs over, the one named last changes fastest.
Arguments:
- initial_states: float32 [8, 8, 64, 256], P('tm', None, 'sx', 'sy'), may hold values from -6 to 6
- coarse_decay: float32 [8, 8, 64, 256], P('tm', None, 'sx', 'sy'), may hold values from 0 to 1, as said below
- power_map: float32 [8, 64, 256], P(None, 'sx', 'sy'), may hold values from 0.5 to 2
- power_mask: int32 [8, 4, 8], P('tm'), may hold values 0 or 1
- region_ids: int32 [8, 8], replicated, may hold values from 0 to 3
- region_conductivity: float32 [4], replicated, may hold values from 0.4 to 2.5
Outputs:
- cycle_states: float32 [8, 8, 64, 256], P('tm', None, 'sx', 'sy')
- jump_field: float32 [8, 8, 64, 256], P('tm', None, 'sx', 'sy')
Inputs may be any that keep to these rules, and one draw needn't show every extreme that they name: `coarse_decay`: every entry lies between 0 and 1, and for every cell the product of its 8 factors is at most one half.
All inputs are finite; a program needn't handle non-finite values. No bound on the sum of `power_mask` on one device may be relied on, other than what follows from the above.
Results may differ from a plain program's by a relative error of at most 0.0001.
Values sent between devices are 32-bit elements; how exact they have to be, the bound alone decides.
A program may use at most 128 MiB of HBM per device.

v0:
```python
import jax
import jax.numpy as jnp
from jax import lax
from jax.sharding import PartitionSpec as P

RB = 8
REGIONS = 4
FSTEPS = 4
SWEEPS = 3
ITERS = 2


grid_xy = 1.0
grid_z = 0.5
sink_gain = 0.5
source_gain = 0.5
cond_slope = 0.25
joule_slope = 0.3


def padded_2(x, sides, width):
    for axis, dim in sides:
        peers, length = (lax.axis_size(axis), x.shape[dim])
        up = [(i, (i + 1) % peers) for i in range(peers - 1)]
        down = [(j, i) for i, j in up]
        last = lax.slice_in_dim(x, length - width, length, axis=dim)
        initial = lax.slice_in_dim(x, 0, width, axis=dim)
        before = lax.ppermute(last, axis, up)
        after = lax.ppermute(initial, axis, down)
        x = jnp.concatenate([before, x, after], axis=dim)
    return x


def entering(x, axis, combine, identity):
    peers, here = (lax.axis_size(axis), lax.axis_index(axis))
    everything = jax.tree.map(lambda part: lax.all_gather(part, axis), x)
    start = jax.tree.map(
        lambda part, zero: jnp.broadcast_to(jnp.asarray(zero, part.dtype), part.shape), x, identity
    )

    def step(k, before):
        reached = k < here
        new = combine(before, jax.tree.map(lambda part: part[k], everything))
        return jax.tree.map(lambda a, b: jnp.where(reached, a, b), new, before)

    return lax.fori_loop(0, peers, step, start)


def broadcast(x, axis, root):
    mine = lax.axis_index(axis) == root
    return lax.psum(jnp.where(mine, x, jnp.zeros_like(x)), axis)


def passed_along(block, axis, distance):
    devices = range(lax.axis_size(axis))
    route = [((i - distance) % len(devices), i) for i in devices]
    return lax.ppermute(block, axis, route)


def base_rows(region_ids, region_conductivity):
    labels = jnp.arange(REGIONS, dtype=jnp.int32)
    chosen = (region_ids[:, :, None] == labels[None, None, :]).astype(jnp.float32)
    return jnp.sum(chosen * region_conductivity[None, None, :], axis=2)


def face_weights(cond_pad, weight_scale):
    middle = cond_pad[:, 1:-1, 1:-1]
    layer_index = lax.broadcasted_iota(jnp.int32, middle.shape, 0)
    blank_layer = jnp.zeros_like(middle[:1])
    layer_above = jnp.concatenate([middle[1:], blank_layer], axis=0)
    layer_below = jnp.concatenate([blank_layer, middle[:-1]], axis=0)
    weight_west = weight_scale * (grid_xy * (0.5 * (middle + cond_pad[:, :-2, 1:-1])))
    weight_east = weight_scale * (grid_xy * (0.5 * (middle + cond_pad[:, 2:, 1:-1])))
    weight_south = weight_scale * (grid_xy * (0.5 * (middle + cond_pad[:, 1:-1, :-2])))
    weight_north = weight_scale * (grid_xy * (0.5 * (middle + cond_pad[:, 1:-1, 2:])))
    weight_up = jnp.where(
        layer_index == middle.shape[0] - 1,
        jnp.zeros_like(middle),
        weight_scale * (grid_z * (0.5 * (middle + layer_above))),
    )
    weight_down = jnp.where(
        layer_index == 0,
        weight_scale * (sink_gain * middle),
        weight_scale * (grid_z * (0.5 * (middle + layer_below))),
    )
    denominator = 1.0 + (
        weight_west + weight_east + weight_south + weight_north + weight_down + weight_up
    )
    return (
        (weight_west, weight_east, weight_south, weight_north, weight_down, weight_up),
        denominator,
    )


def relax(padded, weights, right_side, denominator):
    weight_west, weight_east, weight_south, weight_north, weight_down, weight_up = weights
    middle = padded[:, 1:-1, 1:-1]
    blank_layer = jnp.zeros_like(middle[:1])
    layer_above = jnp.concatenate([middle[1:], blank_layer], axis=0)
    layer_below = jnp.concatenate([blank_layer, middle[:-1]], axis=0)
    summed = weight_west * padded[:, :-2, 1:-1] + weight_east * padded[:, 2:, 1:-1]
    summed = summed + weight_south * padded[:, 1:-1, :-2] + weight_north * padded[:, 1:-1, 2:]
    summed = summed + weight_down * layer_below + weight_up * layer_above
    return (right_side + summed) / denominator


def compose_forward(earlier, later):
    return (earlier[0] * later[0], later[0] * earlier[1] + later[1])


def shards(initial_states, coarse_decay, power_map, power_mask, region_ids, region_conductivity):
    tile_rows = initial_states.shape[2]
    tile_cols = initial_states.shape[3]
    block_count = region_ids.shape[1]
    row_first = lax.axis_index("sx") * tile_rows
    col_first = lax.axis_index("sy") * tile_cols
    grid_rows = tile_rows * lax.axis_size("sx")
    grid_cols = tile_cols * lax.axis_size("sy")
    per_block = base_rows(region_ids, region_conductivity)
    mask_blocks = power_mask[0].astype(jnp.float32)
    row_ids = row_first - 1 + jnp.arange(tile_rows + 2 * 1, dtype=jnp.int32)
    col_ids = col_first - 1 + jnp.arange(tile_cols + 2 * 1, dtype=jnp.int32)
    row_inside = ((row_ids >= 0) & (row_ids < grid_rows)).astype(jnp.float32)
    col_inside = ((col_ids >= 0) & (col_ids < grid_cols)).astype(jnp.float32)
    block_of = jnp.clip(row_ids // RB, 0, block_count - 1)
    block_hit = (block_of[:, None] == jnp.arange(block_count, dtype=jnp.int32)[None, :]).astype(
        jnp.float32
    )
    base_cond = jnp.sum(per_block[:, None, :] * block_hit[None, :, :], axis=2)
    mask_rows = jnp.sum(mask_blocks[:, None, :] * block_hit[None, :, :], axis=2)
    inside = row_inside[None, :, None] * col_inside[None, None, :]
    decay_rate = coarse_decay[0]
    states = initial_states[0]
    jump_field = jnp.zeros_like(states)
    for round_index in range(ITERS):
        current = states
        previous = states
        for substep in range(FSTEPS):
            if substep == 0:
                coef_now, coef_old, weight_scale = (1.0, 0.0, 1.0)
            else:
                coef_now, coef_old, weight_scale = (4.0 / 3.0, -1.0 / 3.0, 2.0 / 3.0)
            iterate = current
            for sweep_index in range(SWEEPS):
                padded = padded_2(iterate, (("sx", 1), ("sy", 2)), 1)
                if sweep_index == 0:
                    conductance = (
                        base_cond[:, :, None] * (1.0 - cond_slope * jnp.tanh(padded)) * inside
                    )
                    weights, denominator = face_weights(conductance, weight_scale)
                    heat_source = (
                        source_gain
                        * mask_rows[substep][1:-1][None, :, None]
                        * power_map
                        * (1.0 + joule_slope * jnp.tanh(current))
                    )
                    right_side = (
                        coef_now * current + coef_old * previous + weight_scale * heat_source
                    )
                iterate = relax(padded, weights, right_side, denominator)
            previous = current
            current = iterate
        if round_index == ITERS - 1:
            following = passed_along(states, "tm", -1)
            jump_field = current - following
        offset = current - decay_rate * states
        unit_map = jnp.ones_like(decay_rate)
        zero_map = jnp.zeros_like(decay_rate)
        scale_pre, shift_pre = entering(
            (decay_rate, offset), "tm", compose_forward, (unit_map, zero_map)
        )
        scale_incl = scale_pre * decay_rate
        shift_incl = decay_rate * shift_pre + offset
        scale_total = broadcast(scale_incl, "tm", lax.axis_size("tm") - 1)
        shift_total = broadcast(shift_incl, "tm", lax.axis_size("tm") - 1)
        first_state = shift_total / (1.0 - scale_total)
        states = scale_pre * first_state + shift_pre
    return (states[None], jump_field[None])


def solution(mesh):
    return jax.shard_map(
        shards,
        mesh=mesh,
        in_specs=(
            P("tm", None, "sx", "sy"),
            P("tm", None, "sx", "sy"),
            P(None, "sx", "sy"),
            P("tm", None, None),
            P(),
            P(),
        ),
        out_specs=(P("tm", None, "sx", "sy"), P("tm", None, "sx", "sy")),
        check_vma=False,
    )
```

profile of v0, /device:TPU:0, one launch (start us, length us, event | category | flops | bytes accessed | tf_op | source)
XLA Modules:
  0.0 630.7 jit_solution(6579108900131379614)
XLA Ops:
  14.7 4.3 collective-permute-start.2
  23.3 4.4 collective-permute-done.3
  39.8 4.1 collective-permute-done.7
  54.2 4.1 collective-permute-done.11
  68.6 4.1 collective-permute-done.15
  83.4 4.1 collective-permute-done.19
  97.7 4.1 collective-permute-done.23
  112.1 4.1 collective-permute-done.27
  126.9 4.1 collective-permute-done.31
  141.3 4.1 collective-permute-done.35
  155.7 4.1 collective-permute-done.39
  170.5 4.1 collective-permute-done.43
  184.9 4.3 collective-permute-done.47
  190.3 14.4 %all-gather.6.cloned.1.call-done = f32[8,8,32,128]{3,2,1,0:T(8,128)} async-done(((f32[1,8,32,128]{3,2,1,0:T(8,128)}), f32[8,8,32,128]{3,2,1,0:T(8,128)}) %all-gather.6.cloned.1.call-update) | async-done | bytes 1048592 | tf_op jit(solution)/shard_map/all_gather | solution.py:36
  204.7 41.6 %all-gather.8.cloned.1.call-done = f32[64,32,128]{2,1,0:T(8,128)} async-done(((f32[8,32,128]{2,1,0:T(8,128)}), f32[64,32,128]{2,1,0:T(8,128)}) %all-gather.8.cloned.1.call-update) | async-done | bytes 1048592 | tf_op jit(solution)/shard_map/all_gather | solution.py:36
  246.3 8.8 %while.32 = (s32[]{:T(128)}, f32[8,32,128]{2,1,0:T(8,128)S(1)}, f32[8,32,128]{2,1,0:T(8,128)S(1)}, s32[]{:T(128)}, f32[8,8,32,128]{3,2,1,0:T(8,128)}, /*index=5*/f32[8,8,32,128]{3,2,1,0:T(8,128)}, s32[]{:T(128)}, s32[]{:T(128)}) while((s32[]{:T(128)}, f32[8,32,128]{2,1,0:T(8,128)S(1)}, f32[8,32,128]{2,1,0:T(8,128)S(1)}, s32[]{:T(128)}, ...), condition=%wide.region_4.5_spmd.clone, body=%wide.region_3.4_spmd.clone.sunk | while | flops 229380 | bytes 786541 | solution.py:46
  255.9 69.7 %all-reduce.71.cloned.1.call-done = (f32[8,32,128]{2,1,0:T(8,128)}, f32[8,32,128]{2,1,0:T(8,128)}) async-done(((f32[8,32,128]{2,1,0:T(8,128)}, f32[8,32,128]{2,1,0:T(8,128)}), (f32[8,32,128]{2,1,0:T(8,128)}, f32[8,32,128]{2,1,0:T(8,128)})) %all-reduce.71.cloned.1.call-update) | async-done | bytes 262160 | tf_op jit(solution)/shard_map/psum | solution.py:51
  338.3 4.1 collective-permute-done.51
  353.1 4.1 collective-permute-done.55
  367.5 4.1 collective-permute-done.59
  381.9 4.1 collective-permute-done.63
  396.7 4.1 collective-permute-done.67
  411.1 4.1 collective-permute-done.71
  425.5 4.1 collective-permute-done.75
  440.3 4.1 collective-permute-done.79
  454.7 4.1 collective-permute-done.83
  469.0 4.1 collective-permute-done.87
  483.9 4.1 collective-permute-done.91
  499.8 4.1 collective-permute-done.95
  505.8 37.5 %all-gather.10.cloned.1.call-done = f32[64,32,128]{2,1,0:T(8,128)} async-done(((f32[8,32,128]{2,1,0:T(8,128)}), f32[64,32,128]{2,1,0:T(8,128)}) %all-gather.10.cloned.1.call-update) | async-done | bytes 1048592 | tf_op jit(solution)/shard_map/all_gather | solution.py:36
  543.2 8.8 %while.33 = (s32[]{:T(128)}, f32[8,32,128]{2,1,0:T(8,128)S(1)}, f32[8,32,128]{2,1,0:T(8,128)S(1)}, s32[]{:T(128)}, f32[8,8,32,128]{3,2,1,0:T(8,128)}, /*index=5*/f32[8,8,32,128]{3,2,1,0:T(8,128)}, s32[]{:T(128)}, s32[]{:T(128)}) while((s32[]{:T(128)}, f32[8,32,128]{2,1,0:T(8,128)S(1)}, f32[8,32,128]{2,1,0:T(8,128)S(1)}, s32[]{:T(128)}, ...), condition=%wide.region_8.9_spmd.clone, body=%wide.region_7.8_spmd.clone.sunk | while | flops 229380 | bytes 786541 | solution.py:46
  552.8 69.7 %all-reduce.69.cloned.1.call-done = (f32[8,32,128]{2,1,0:T(8,128)}, f32[8,32,128]{2,1,0:T(8,128)}) async-done(((f32[8,32,128]{2,1,0:T(8,128)}, f32[8,32,128]{2,1,0:T(8,128)}), (f32[8,32,128]{2,1,0:T(8,128)}, f32[8,32,128]{2,1,0:T(8,128)})) %all-reduce.69.cloned.1.call-update) | async-done | bytes 262160 | tf_op jit(solution)/shard_map/psum | solution.py:51
  (367 shorter events, 278.1 us)
Async XLA Ops:
  7.2 197.5 %all-gather.6.cloned.1.call-start = ((), (), s32[]{:S(2)}) async-start(), calls=%async_computation | async-start | bytes 1179648 | tf_op jit(solution)/shard_map/all_gather | solution.py:36
  14.7 8.7 %collective-permute-start.2 = (f32[8,34,1]{2,1,0:T(8,128)S(1)}, f32[8,34,1]{2,1,0:T(8,128)S(1)}, u32[]{:S(2)}, u32[]{:S(2)}) collective-permute-start(f32[8,34,1]{2,1,0:T(8,128)S(1)} %get-tuple-element.378), channel_id=1, source_target_pairs={{0,1},{2,3},{4,5},{6,7},{8,9},{10,11},{12,13},{14,15},{16,17},{18,... | collective-permute-start | bytes 3272 | tf_op jit(solution)/shard_map/ppermute | solution.py:28
  18.9 8.8 %collective-permute-start.3 = (f32[8,34,1]{2,1,0:T(8,128)S(1)}, f32[8,34,1]{2,1,0:T(8,128)S(1)}, u32[]{:S(2)}, u32[]{:S(2)}) collective-permute-start(f32[8,34,1]{2,1,0:T(8,128)S(1)} %get-tuple-element.379), channel_id=1, source_target_pairs={{1,0},{3,2},{5,4},{7,6},{9,8},{11,10},{13,12},{15,14},{17,16},{19,... | collective-permute-start | bytes 3272 | tf_op jit(solution)/shard_map/ppermute | solution.py:29
  36.0 8.0 %collective-permute-start.7 = (f32[8,34,1]{2,1,0:T(8,128)S(1)}, f32[8,34,1]{2,1,0:T(8,128)S(1)}, u32[]{:S(2)}, u32[]{:S(2)}) collective-permute-start(f32[8,34,1]{2,1,0:T(8,128)S(1)} %get-tuple-element.377), channel_id=1, source_target_pairs={{1,0},{3,2},{5,4},{7,6},{9,8},{11,10},{13,12},{15,14},{17,16},{19,... | collective-permute-start | bytes 3272 | tf_op jit(solution)/shard_map/ppermute | solution.py:29
  50.3 8.0 %collective-permute-start.11 = (f32[8,34,1]{2,1,0:T(8,128)S(1)}, f32[8,34,1]{2,1,0:T(8,128)S(1)}, u32[]{:S(2)}, u32[]{:S(2)}) collective-permute-start(f32[8,34,1]{2,1,0:T(8,128)S(1)} %get-tuple-element.375), channel_id=1, source_target_pairs={{1,0},{3,2},{5,4},{7,6},{9,8},{11,10},{13,12},{15,14},{17,16},{19,... | collective-permute-start | bytes 3272 | tf_op jit(solution)/shard_map/ppermute | solution.py:29
  64.7 8.0 %collective-permute-start.15 = (f32[8,34,1]{2,1,0:T(8,128)S(1)}, f32[8,34,1]{2,1,0:T(8,128)S(1)}, u32[]{:S(2)}, u32[]{:S(2)}) collective-permute-start(f32[8,34,1]{2,1,0:T(8,128)S(1)} %get-tuple-element.373), channel_id=1, source_target_pairs={{1,0},{3,2},{5,4},{7,6},{9,8},{11,10},{13,12},{15,14},{17,16},{19,... | collective-permute-start | bytes 3272 | tf_op jit(solution)/shard_map/ppermute | solution.py:29
  79.5 8.0 %collective-permute-start.19 = (f32[8,34,1]{2,1,0:T(8,128)S(1)}, f32[8,34,1]{2,1,0:T(8,128)S(1)}, u32[]{:S(2)}, u32[]{:S(2)}) collective-permute-start(f32[8,34,1]{2,1,0:T(8,128)S(1)} %get-tuple-element.371), channel_id=1, source_target_pairs={{1,0},{3,2},{5,4},{7,6},{9,8},{11,10},{13,12},{15,14},{17,16},{19,... | collective-permute-start | bytes 3272 | tf_op jit(solution)/shard_map/ppermute | solution.py:29
  93.9 8.0 %collective-permute-start.23 = (f32[8,34,1]{2,1,0:T(8,128)S(1)}, f32[8,34,1]{2,1,0:T(8,128)S(1)}, u32[]{:S(2)}, u32[]{:S(2)}) collective-permute-start(f32[8,34,1]{2,1,0:T(8,128)S(1)} %get-tuple-element.369), channel_id=1, source_target_pairs={{1,0},{3,2},{5,4},{7,6},{9,8},{11,10},{13,12},{15,14},{17,16},{19,... | collective-permute-start | bytes 3272 | tf_op jit(solution)/shard_map/ppermute | solution.py:29
  108.2 8.0 %collective-permute-start.27 = (f32[8,34,1]{2,1,0:T(8,128)S(1)}, f32[8,34,1]{2,1,0:T(8,128)S(1)}, u32[]{:S(2)}, u32[]{:S(2)}) collective-permute-start(f32[8,34,1]{2,1,0:T(8,128)S(1)} %get-tuple-element.367), channel_id=1, source_target_pairs={{1,0},{3,2},{5,4},{7,6},{9,8},{11,10},{13,12},{15,14},{17,16},{19,... | collective-permute-start | bytes 3272 | tf_op jit(solution)/shard_map/ppermute | solution.py:29
  123.1 8.0 %collective-permute-start.31 = (f32[8,34,1]{2,1,0:T(8,128)S(1)}, f32[8,34,1]{2,1,0:T(8,128)S(1)}, u32[]{:S(2)}, u32[]{:S(2)}) collective-permute-start(f32[8,34,1]{2,1,0:T(8,128)S(1)} %get-tuple-element.365), channel_id=1, source_target_pairs={{1,0},{3,2},{5,4},{7,6},{9,8},{11,10},{13,12},{15,14},{17,16},{19,... | collective-permute-start | bytes 3272 | tf_op jit(solution)/shard_map/ppermute | solution.py:29
  137.4 8.0 %collective-permute-start.35 = (f32[8,34,1]{2,1,0:T(8,128)S(1)}, f32[8,34,1]{2,1,0:T(8,128)S(1)}, u32[]{:S(2)}, u32[]{:S(2)}) collective-permute-start(f32[8,34,1]{2,1,0:T(8,128)S(1)} %get-tuple-element.363), channel_id=1, source_target_pairs={{1,0},{3,2},{5,4},{7,6},{9,8},{11,10},{13,12},{15,14},{17,16},{19,... | collective-permute-start | bytes 3272 | tf_op jit(solution)/shard_map/ppermute | solution.py:29
  151.8 8.0 %collective-permute-start.39 = (f32[8,34,1]{2,1,0:T(8,128)S(1)}, f32[8,34,1]{2,1,0:T(8,128)S(1)}, u32[]{:S(2)}, u32[]{:S(2)}) collective-permute-start(f32[8,34,1]{2,1,0:T(8,128)S(1)} %get-tuple-element.361), channel_id=1, source_target_pairs={{1,0},{3,2},{5,4},{7,6},{9,8},{11,10},{13,12},{15,14},{17,16},{19,... | collective-permute-start | bytes 3272 | tf_op jit(solution)/shard_map/ppermute | solution.py:29
  163.3 83.0 %all-gather.8.cloned.1.call-start = ((), (), s32[]{:S(2)}) async-start(), calls=%async_computation.1 | async-start | bytes 1179648 | tf_op jit(solution)/shard_map/all_gather | solution.py:36
  166.6 8.0 %collective-permute-start.43 = (f32[8,34,1]{2,1,0:T(8,128)S(1)}, f32[8,34,1]{2,1,0:T(8,128)S(1)}, u32[]{:S(2)}, u32[]{:S(2)}) collective-permute-start(f32[8,34,1]{2,1,0:T(8,128)S(1)} %get-tuple-element.359), channel_id=1, source_target_pairs={{1,0},{3,2},{5,4},{7,6},{9,8},{11,10},{13,12},{15,14},{17,16},{19,... | collective-permute-start | bytes 3272 | tf_op jit(solution)/shard_map/ppermute | solution.py:29
  181.0 8.1 %collective-permute-start.47 = (f32[8,34,1]{2,1,0:T(8,128)S(1)}, f32[8,34,1]{2,1,0:T(8,128)S(1)}, u32[]{:S(2)}, u32[]{:S(2)}) collective-permute-start(f32[8,34,1]{2,1,0:T(8,128)S(1)} %get-tuple-element.357), channel_id=1, source_target_pairs={{1,0},{3,2},{5,4},{7,6},{9,8},{11,10},{13,12},{15,14},{17,16},{19,... | collective-permute-start | bytes 3272 | tf_op jit(solution)/shard_map/ppermute | solution.py:29
  190.2 135.4 %all-reduce.71.cloned.1.call-start = ((), (), s32[]{:S(2)}) async-start(), calls=%async_computation.4 | async-start | bytes 524288 | tf_op jit(solution)/shard_map/psum | solution.py:51
  255.9 287.4 %all-gather.10.cloned.1.call-start = ((), (), s32[]{:S(2)}) async-start(), calls=%async_computation.2 | async-start | bytes 1179648 | tf_op jit(solution)/shard_map/all_gather | solution.py:36
  331.1 7.2 %collective-permute-start.50 = (f32[8,34,1]{2,1,0:T(8,128)S(1)}, f32[8,34,1]{2,1,0:T(8,128)S(1)}, u32[]{:S(2)}, u32[]{:S(2)}) collective-permute-start(f32[8,34,1]{2,1,0:T(8,128)S(1)} %get-tuple-element.354), channel_id=1, source_target_pairs={{0,1},{2,3},{4,5},{6,7},{8,9},{10,11},{12,13},{14,15},{16,17},{18,... | collective-permute-start | bytes 3272 | tf_op jit(solution)/shard_map/ppermute | solution.py:28
  334.5 7.9 %collective-permute-start.51 = (f32[8,34,1]{2,1,0:T(8,128)S(1)}, f32[8,34,1]{2,1,0:T(8,128)S(1)}, u32[]{:S(2)}, u32[]{:S(2)}) collective-permute-start(f32[8,34,1]{2,1,0:T(8,128)S(1)} %get-tuple-element.355), channel_id=1, source_target_pairs={{1,0},{3,2},{5,4},{7,6},{9,8},{11,10},{13,12},{15,14},{17,16},{19,... | collective-permute-start | bytes 3272 | tf_op jit(solution)/shard_map/ppermute | solution.py:29
  349.2 8.0 %collective-permute-start.55 = (f32[8,34,1]{2,1,0:T(8,128)S(1)}, f32[8,34,1]{2,1,0:T(8,128)S(1)}, u32[]{:S(2)}, u32[]{:S(2)}) collective-permute-start(f32[8,34,1]{2,1,0:T(8,128)S(1)} %get-tuple-element.353), channel_id=1, source_target_pairs={{1,0},{3,2},{5,4},{7,6},{9,8},{11,10},{13,12},{15,14},{17,16},{19,... | collective-permute-start | bytes 3272 | tf_op jit(solution)/shard_map/ppermute | solution.py:29
  363.6 8.0 %collective-permute-start.59 = (f32[8,34,1]{2,1,0:T(8,128)S(1)}, f32[8,34,1]{2,1,0:T(8,128)S(1)}, u32[]{:S(2)}, u32[]{:S(2)}) collective-permute-start(f32[8,34,1]{2,1,0:T(8,128)S(1)} %get-tuple-element.351), channel_id=1, source_target_pairs={{1,0},{3,2},{5,4},{7,6},{9,8},{11,10},{13,12},{15,14},{17,16},{19,... | collective-permute-start | bytes 3272 | tf_op jit(solution)/shard_map/ppermute | solution.py:29
  378.0 8.0 %collective-permute-start.63 = (f32[8,34,1]{2,1,0:T(8,128)S(1)}, f32[8,34,1]{2,1,0:T(8,128)S(1)}, u32[]{:S(2)}, u32[]{:S(2)}) collective-permute-start(f32[8,34,1]{2,1,0:T(8,128)S(1)} %get-tuple-element.349), channel_id=1, source_target_pairs={{1,0},{3,2},{5,4},{7,6},{9,8},{11,10},{13,12},{15,14},{17,16},{19,... | collective-permute-start | bytes 3272 | tf_op jit(solution)/shard_map/ppermute | solution.py:29
  392.9 8.0 %collective-permute-start.67 = (f32[8,34,1]{2,1,0:T(8,128)S(1)}, f32[8,34,1]{2,1,0:T(8,128)S(1)}, u32[]{:S(2)}, u32[]{:S(2)}) collective-permute-start(f32[8,34,1]{2,1,0:T(8,128)S(1)} %get-tuple-element.347), channel_id=1, source_target_pairs={{1,0},{3,2},{5,4},{7,6},{9,8},{11,10},{13,12},{15,14},{17,16},{19,... | collective-permute-start | bytes 3272 | tf_op jit(solution)/shard_map/ppermute | solution.py:29
  407.2 8.0 %collective-permute-start.71 = (f32[8,34,1]{2,1,0:T(8,128)S(1)}, f32[8,34,1]{2,1,0:T(8,128)S(1)}, u32[]{:S(2)}, u32[]{:S(2)}) collective-permute-start(f32[8,34,1]{2,1,0:T(8,128)S(1)} %get-tuple-element.345), channel_id=1, source_target_pairs={{1,0},{3,2},{5,4},{7,6},{9,8},{11,10},{13,12},{15,14},{17,16},{19,... | collective-permute-start | bytes 3272 | tf_op jit(solution)/shard_map/ppermute | solution.py:29
  421.6 8.0 %collective-permute-start.75 = (f32[8,34,1]{2,1,0:T(8,128)S(1)}, f32[8,34,1]{2,1,0:T(8,128)S(1)}, u32[]{:S(2)}, u32[]{:S(2)}) collective-permute-start(f32[8,34,1]{2,1,0:T(8,128)S(1)} %get-tuple-element.343), channel_id=1, source_target_pairs={{1,0},{3,2},{5,4},{7,6},{9,8},{11,10},{13,12},{15,14},{17,16},{19,... | collective-permute-start | bytes 3272 | tf_op jit(solution)/shard_map/ppermute | solution.py:29
  436.4 8.0 %collective-permute-start.79 = (f32[8,34,1]{2,1,0:T(8,128)S(1)}, f32[8,34,1]{2,1,0:T(8,128)S(1)}, u32[]{:S(2)}, u32[]{:S(2)}) collective-permute-start(f32[8,34,1]{2,1,0:T(8,128)S(1)} %get-tuple-element.341), channel_id=1, source_target_pairs={{1,0},{3,2},{5,4},{7,6},{9,8},{11,10},{13,12},{15,14},{17,16},{19,... | collective-permute-start | bytes 3272 | tf_op jit(solution)/shard_map/ppermute | solution.py:29
  450.8 8.0 %collective-permute-start.83 = (f32[8,34,1]{2,1,0:T(8,128)S(1)}, f32[8,34,1]{2,1,0:T(8,128)S(1)}, u32[]{:S(2)}, u32[]{:S(2)}) collective-permute-start(f32[8,34,1]{2,1,0:T(8,128)S(1)} %get-tuple-element.339), channel_id=1, source_target_pairs={{1,0},{3,2},{5,4},{7,6},{9,8},{11,10},{13,12},{15,14},{17,16},{19,... | collective-permute-start | bytes 3272 | tf_op jit(solution)/shard_map/ppermute | solution.py:29
  465.1 8.0 %collective-permute-start.87 = (f32[8,34,1]{2,1,0:T(8,128)S(1)}, f32[8,34,1]{2,1,0:T(8,128)S(1)}, u32[]{:S(2)}, u32[]{:S(2)}) collective-permute-start(f32[8,34,1]{2,1,0:T(8,128)S(1)} %get-tuple-element.337), channel_id=1, source_target_pairs={{1,0},{3,2},{5,4},{7,6},{9,8},{11,10},{13,12},{15,14},{17,16},{19,... | collective-permute-start | bytes 3272 | tf_op jit(solution)/shard_map/ppermute | solution.py:29
  480.0 8.0 %collective-permute-start.91 = (f32[8,34,1]{2,1,0:T(8,128)S(1)}, f32[8,34,1]{2,1,0:T(8,128)S(1)}, u32[]{:S(2)}, u32[]{:S(2)}) collective-permute-start(f32[8,34,1]{2,1,0:T(8,128)S(1)} %get-tuple-element.335), channel_id=1, source_target_pairs={{1,0},{3,2},{5,4},{7,6},{9,8},{11,10},{13,12},{15,14},{17,16},{19,... | collective-permute-start | bytes 3272 | tf_op jit(solution)/shard_map/ppermute | solution.py:29
  491.0 13.0 %collective-permute-start.96 = (f32[8,32,128]{2,1,0:T(8,128)S(1)}, f32[8,32,128]{2,1,0:T(8,128)S(1)}, u32[]{:S(2)}, u32[]{:S(2)}) collective-permute-start(f32[8,32,128]{2,1,0:T(8,128)S(1)} %multiply_add_fusion.5), channel_id=1, source_target_pairs={{4,0},{8,4},{12,8},{16,12},{20,16},{24,20},{28,24},{0,28},{5,1},{9... | collective-permute-start | bytes 393224 | tf_op jit(solution)/shard_map/ppermute | solution.py:57
  495.3 8.7 %collective-permute-start.95 = (f32[8,34,1]{2,1,0:T(8,128)S(1)}, f32[8,34,1]{2,1,0:T(8,128)S(1)}, u32[]{:S(2)}, u32[]{:S(2)}) collective-permute-start(f32[8,34,1]{2,1,0:T(8,128)S(1)} %get-tuple-element.333), channel_id=1, source_target_pairs={{1,0},{3,2},{5,4},{7,6},{9,8},{11,10},{13,12},{15,14},{17,16},{19,... | collective-permute-start | bytes 3272 | tf_op jit(solution)/shard_map/ppermute | solution.py:29
  505.7 116.8 %all-reduce.69.cloned.1.call-start = ((), (), s32[]{:S(2)}) async-start(), calls=%async_computation.3 | async-start | bytes 524288 | tf_op jit(solution)/shard_map/psum | solution.py:51
  (78 other events, 295.0 us)
Sparse Core Ops, SparseCore 0:
  163.4 41.2 all-gather.5
  207.3 38.8 all-gather.7
  256.0 69.6 all-reduce.70
  505.8 37.3 all-gather.9
  552.9 69.5 all-reduce.68
where the time goes:
time: 633 us; the launch traced here: 631 us
  waiting for transfers between devices  433 us (68%)
  starting transfers between devices  137 us (22%)
  other arithmetic  36.1 us (6%)
  between operations  15.8 us (2%)
  local copies, waits for them, and re-layouts  7.86 us (1%)
    psum x2, waiting for transfers between devices, broadcast(): return lax.psum(jnp.where(mine, x, jnp.zeros_like(x)), axis)  139 us
    ppermute x48, waiting for transfers between devices, padded_2(): after = lax.ppermute(initial, axis, down)  138 us
    all_gather x3, waiting for transfers between devices, entering(): everything = jax.tree.map(lambda part: lax.all_gather(part, axis), x)  93.5 us
    ppermute x48, starting transfers between devices, padded_2(): before = lax.ppermute(last, axis, up)  72.3 us
    ppermute x48, waiting for transfers between devices, padded_2(): before = lax.ppermute(last, axis, up)  62.4 us
    ppermute x48, starting transfers between devices, padded_2(): after = lax.ppermute(initial, axis, down)  62.2 us
    select_n x16, other arithmetic, step(): return jax.tree.map(lambda a, b: jnp.where(reached, a, b), new, before)  17.2 us
  transfers between devices with their start and end apart: 102, of which 75 were waited for; matrix products, arithmetic and copies ran while one was open for 1% of the time, Pallas kernels for 0%

commit v1 on v0

v1 whole, which is shorter than its diff:
```python
import functools

import jax
import jax.numpy as jnp
from jax import lax
from jax.experimental import pallas as pl
from jax.experimental.pallas import tpu as pltpu
from jax.sharding import PartitionSpec as P

RB = 8
FSTEPS = 4
SWEEPS = 3
ITERS = 2
LAYERS = 8
ROWS = 32
COLS = 128
HALO = FSTEPS * SWEEPS
EXT = ROWS + HALO
PAD = 48
STRIP = 16
BLOCK = 4

cond_slope = 0.25
joule_slope = 0.3
MESH = pl.DeviceIdType.MESH


def kernel(
    slabs, solvers, chunk,
    state_ref, decay_ref, power_ref, mask_ref, ids_ref, cond_ref,
    out_ref, jump_ref,
    own, dec, off, packed, rows_in, side_in, corner_in,
    v, cond, rhs, wx, wy, wz, rden, power, base,
    a_in, b_in, u_out, u_in,
    near_send, near_recv, far_send, far_recv,
):
    tm, sx, sy = lax.axis_index("tm"), lax.axis_index("sx"), lax.axis_index("sy")
    other_core, side, corner = (tm, 1 - sx, sy), (tm, sx, 1 - sy), (tm, 1 - sx, 1 - sy)

    def slab_at(distance):
        return lax.rem(tm + distance, slabs)

    barrier = pltpu.get_barrier_semaphore()
    for peer in (other_core, side, corner):
        pl.semaphore_signal(barrier, inc=1, device_id=peer, device_id_type=MESH)
    for d in range(1, slabs):
        pl.semaphore_signal(barrier, inc=1, device_id=(slab_at(d), sx, sy), device_id_type=MESH)

    def grid_row(r):
        return r + sx * (ROWS - 1 - 2 * r)

    def grid_block(i):
        return i + sx * (ids_ref.shape[1] - 1 - 2 * i)

    lane = lax.broadcasted_iota(jnp.int32, (LAYERS, COLS), 1)
    window = lax.rem(lane // STRIP + 8, 8)
    edge_window = 7 * (1 - sy)

    def pack(slot, kind):
        for g in range(ROWS // 8):
            total = own[kind, 8 * g] if slot is None else u_in[slot, 8 * g]
            for i in range(1, 8):
                row = own[kind, 8 * g + i] if slot is None else u_in[slot, 8 * g + i]
                here = lax.rem(window - i + 8, 8) == edge_window
                total = jnp.where(here, pltpu.roll(row, STRIP * i, 1), total)
            packed[kind if slot is None else 2, g] = total

    def load_rows(r, carry):
        at = pl.ds(grid_row(r), LAYERS, ROWS)
        own[0, r] = state_ref[at, :]
        own[1, r] = power_ref[at, :]
        dec[r] = decay_ref[at, :]
        return carry

    lax.fori_loop(0, ROWS, load_rows, 0, unroll=True)
    pack(None, 0)
    pack(None, 1)

    pl.semaphore_wait(barrier, 3 + slabs - 1)

    def near(src_rows, src_strip, src_corner, slots, k):
        copies = [
            pltpu.make_async_remote_copy(
                src_ref=src, dst_ref=dst, send_sem=near_send.at[k + i], recv_sem=near_recv.at[k + i],
                device_id=peer, device_id_type=MESH,
            )
            for i, (src, dst, peer) in enumerate((
                (src_corner, corner_in.at[slots], corner),
                (src_strip, side_in.at[slots], side),
                (src_rows, rows_in.at[slots], other_core),
            ))
        ]
        for copy in copies:
            copy.start()
        return copies

    first = near(
        own.at[:, pl.ds(ROWS - HALO, HALO)], packed.at[pl.ds(0, 2)],
        packed.at[pl.ds(0, 2), pl.ds(2, 2)], pl.ds(0, 2), 0,
    )

    def to_solvers(src, dst, kind):
        def copy_at(d):
            target = slab_at(d)
            return pltpu.make_async_remote_copy(
                src_ref=src.at[pl.ds(target * chunk, chunk)], dst_ref=dst.at[tm],
                send_sem=far_send.at[kind, d], recv_sem=far_recv.at[kind, d],
                device_id=(target, sx, sy), device_id_type=MESH,
            )

        for d in range(1, slabs):
            guarded(slab_at(d) < solvers, copy_at(d).start)

        def keep():
            dst[tm] = src[pl.ds(tm * chunk, chunk)]

        guarded(tm < solvers, keep)

        def sent():
            for d in range(1, slabs):
                guarded(slab_at(d) < solvers, copy_at(d).wait_send)

        def arrived():
            for d in range(1, slabs):
                copy_at(d).wait_recv()

        return sent, arrived

    def guarded(condition, action):
        if solvers == slabs:
            action()
        else:
            pl.when(condition)(action)

    decay_sent, decay_arrived = to_solvers(dec, a_in, 0)

    blank = jnp.zeros((BLOCK, LAYERS, 2 * COLS), jnp.float32)

    def clear(i, carry):
        at = pl.ds(BLOCK * i, BLOCK)
        for slot in range(3):
            v[slot, at] = blank
        for ref in (cond, rhs, wx, wy, wz, rden, power):
            ref[at] = blank
        return carry

    lax.fori_loop(0, PAD // BLOCK, clear, 0, unroll=True)

    layer = lax.broadcasted_iota(jnp.int32, (LAYERS, 2 * COLS), 0)
    place = lax.broadcasted_iota(jnp.int32, (LAYERS, 2 * COLS), 1)
    for i in range(-(-EXT // RB)):
        block = grid_block(i)
        value = jnp.zeros((LAYERS, 2 * COLS), jnp.float32)
        for l in range(LAYERS):
            value = jnp.where(layer == l, cond_ref[ids_ref[l, block]], value)
        base[i] = value
    first_col = place == sy * COLS
    last_col = place == 2 * COLS - 1 - sy * COLS
    wy_mask = jnp.where(first_col, 0.0, 1.0)
    wz_mask = jnp.where(layer == 0, 0.0, 0.5)
    border = (
        jnp.where(layer == 0, 1.0, 0.0)
        + jnp.where(first_col, 1.0, 0.0)
        + jnp.where(last_col, 1.0, 0.0)
    )

    def spread(store, slot):
        for i in range(HALO):
            store(EXT - 1 - i, 0, rows_in[slot, i])
        for i in range(8):
            for g in range(ROWS // 8):
                store(8 * g + i, 1, pltpu.roll(side_in[slot, g], (COLS - STRIP * i) % COLS, 1))
            for g in range(2):
                r = 2 * ROWS - 1 - (16 + 8 * g + i)
                if r < EXT:
                    store(r, 1, pltpu.roll(corner_in[slot, g], (COLS - STRIP * i) % COLS, 1))

    def store_state(r, half, value):
        v[0, 1 + r, :, half * COLS:(half + 1) * COLS] = value

    def store_power(r, half, value):
        power[1 + r, :, half * COLS:(half + 1) * COLS] = value

    def sweep(source, target, count, with_weights):
        def body(i, carry):
            r = BLOCK * i
            at, before, after = pl.ds(r + 1, BLOCK), pl.ds(r, BLOCK), pl.ds(r + 2, BLOCK)
            if with_weights:
                k = cond[at]
                west = k + cond[before]
                east = k + cond[after]
                south = wy_mask * (k + pltpu.roll(k, 1, 2))
                down = wz_mask * (k + pltpu.roll(k, 1, 1))
                den = 1.0 + (
                    west + east + south + pltpu.roll(south, 2 * COLS - 1, 2)
                    + down + pltpu.roll(down, LAYERS - 1, 1) + border * k
                )
                inverse = 1.0 / den
                wx[at] = west
                wy[at] = south
                wz[at] = down
                rden[at] = inverse
            else:
                west, east, south, down, inverse = wx[at], wx[after], wy[at], wz[at], rden[at]
            mid = v[source, at]
            total = rhs[at] + west * v[source, before] + east * v[source, after]
            total = total + south * pltpu.roll(mid, 1, 2)
            total = total + pltpu.roll(south * mid, 2 * COLS - 1, 2)
            total = total + down * pltpu.roll(mid, 1, 1)
            total = total + pltpu.roll(down * mid, LAYERS - 1, 1)
            v[target, at] = total * inverse
            return carry

        lax.fori_loop(0, -(-count // BLOCK), body, 0, unroll=True)

    def fine():
        now, old, spare = 0, 1, 2
        for m in range(FSTEPS):
            coef_now, coef_old, scale = (1.0, 0.0, 1.0) if m == 0 else (4.0 / 3.0, -1.0 / 3.0, 2.0 / 3.0)
            half = 0.5 * scale
            reach = EXT - SWEEPS * m

            def prepare(i, carry, m=m, now=now, old=old, coef_now=coef_now, coef_old=coef_old, half=half):
                at = pl.ds(BLOCK * i + 1, BLOCK)
                block = (BLOCK * i) // RB
                current = v[now, at]
                t = jnp.tanh(current)
                cond[at] = base[block] * (half - (half * cond_slope) * t)
                on = half * mask_ref[0, m, grid_block(block)].astype(jnp.float32)
                total = (on * power[at]) * (1.0 + joule_slope * t)
                if m == 0:
                    total = total + current
                else:
                    total = total + (coef_now * current + coef_old * v[old, at])
                rhs[at] = total
                return carry

            lax.fori_loop(0, -(-reach // BLOCK), prepare, 0, unroll=True)
            sweep(now, spare, reach - 1, True)
            sweep(spare, old, reach - 2, False)
            sweep(old, spare, reach - 3, False)
            now, old, spare = spare, now, old
        return now

    def solve(it):
        a = [a_in[n] for n in range(slabs)]
        total = b_in[it, 0]
        product = a[0]
        for n in range(1, slabs):
            total = a[n] * total + b_in[it, n]
            product = product * a[n]
        state = total / (1.0 - product)
        for n in range(slabs):
            u_out[it, n] = state
            if n < slabs - 1:
                state = a[n] * state + b_in[it, n]

    def from_solvers(it):
        kind = 1 + ITERS + it

        def copy_at(d):
            target = slab_at(d)
            return pltpu.make_async_remote_copy(
                src_ref=u_out.at[it, target], dst_ref=u_in.at[it, pl.ds(tm * chunk, chunk)],
                send_sem=far_send.at[kind, d], recv_sem=far_recv.at[kind, d],
                device_id=(target, sx, sy), device_id_type=MESH,
            )

        def work():
            solve(it)
            for d in range(1, slabs):
                copy_at(d).start()
            u_in[it, pl.ds(tm * chunk, chunk)] = u_out[it, tm]

        guarded(tm < solvers, work)

        def sent():
            for d in range(1, slabs):
                copy_at(d).wait_send()

        def arrived():
            for d in range(1, slabs):
                guarded(lax.rem(tm - d + slabs, slabs) < solvers, copy_at(d).wait_recv)

        return lambda: guarded(tm < solvers, sent), arrived

    pending = [decay_sent]
    for r in range(ROWS):
        store_state(r, 0, own[0, r])
        store_power(r, 0, own[1, r])
    for copy in first:
        copy.wait_recv()
    pending += [copy.wait_send for copy in first]
    spread(store_state, 0)
    spread(store_power, 1)

    for it in range(ITERS):
        if it:
            for r in range(ROWS):
                store_state(r, 0, u_in[it - 1, r])
            pack(it - 1, 0)
            again = near(
                u_in.at[pl.ds(it - 1, 1), pl.ds(ROWS - HALO, HALO)], packed.at[pl.ds(2, 1)],
                packed.at[pl.ds(2, 1), pl.ds(2, 2)], pl.ds(2, 1), 3,
            )
            for copy in again:
                copy.wait_recv()
            pending += [copy.wait_send for copy in again]
            spread(store_state, 2)
        end = fine()

        def offsets(i, carry, it=it, end=end):
            at = pl.ds(BLOCK * i, BLOCK)
            start = own[0, at] if it == 0 else u_in[it - 1, at]
            off[it, at] = v[end, pl.ds(BLOCK * i + 1, BLOCK), :, 0:COLS] - dec[at] * start
            return carry

        lax.fori_loop(0, ROWS // BLOCK, offsets, 0, unroll=True)
        sent, arrived = to_solvers(off.at[it], b_in.at[it], 1 + it)
        pending.append(sent)
        if it == 0:
            guarded(tm < solvers, decay_arrived)
        if it == ITERS - 1:

            def jumps(r, carry, it=it, end=end):
                following = dec[r] * u_in[it - 1, r] + off[it - 1, r]
                jump_ref[pl.ds(grid_row(r), LAYERS, ROWS), :] = v[end, r + 1, :, 0:COLS] - following
                return carry

            lax.fori_loop(0, ROWS, jumps, 0, unroll=True)
        guarded(tm < solvers, arrived)
        sent, arrived = from_solvers(it)
        pending.append(sent)
        arrived()

    def finish(r, carry):
        out_ref[pl.ds(grid_row(r), LAYERS, ROWS), :] = u_in[ITERS - 1, r]
        return carry

    lax.fori_loop(0, ROWS, finish, 0, unroll=True)
    for wait in pending:
        wait()


def shards(slabs, initial_states, coarse_decay, power_map, power_mask, region_ids, region_conductivity):
    solvers = min(slabs, ROWS)
    chunk = ROWS // solvers
    flat = (LAYERS * ROWS, COLS)
    f32 = jnp.float32
    tile = (ROWS, LAYERS, COLS)
    wide = (PAD, LAYERS, 2 * COLS)
    vmem = pl.BlockSpec(memory_space=pltpu.VMEM)
    smem = pl.BlockSpec(memory_space=pltpu.SMEM)
    kinds = 1 + 2 * ITERS
    states, jump = pl.pallas_call(
        functools.partial(kernel, slabs, solvers, chunk),
        out_shape=[jax.ShapeDtypeStruct(flat, f32)] * 2,
        in_specs=[vmem] * 3 + [smem] * 3,
        out_specs=[vmem] * 2,
        scratch_shapes=[
            pltpu.VMEM((2,) + tile, f32),
            pltpu.VMEM(tile, f32),
            pltpu.VMEM((ITERS,) + tile, f32),
            pltpu.VMEM((3, ROWS // 8, LAYERS, COLS), f32),
            pltpu.VMEM((3, HALO, LAYERS, COLS), f32),
            pltpu.VMEM((3, ROWS // 8, LAYERS, COLS), f32),
            pltpu.VMEM((3, 2, LAYERS, COLS), f32),
            pltpu.VMEM((3,) + wide, f32),
            *[pltpu.VMEM(wide, f32) for _ in range(7)],
            pltpu.VMEM((-(-EXT // RB), LAYERS, 2 * COLS), f32),
            pltpu.VMEM((slabs, chunk, LAYERS, COLS), f32),
            pltpu.VMEM((ITERS, slabs, chunk, LAYERS, COLS), f32),
            pltpu.VMEM((ITERS, slabs, chunk, LAYERS, COLS), f32),
            pltpu.VMEM((ITERS,) + tile, f32),
            pltpu.SemaphoreType.DMA((6,)),
            pltpu.SemaphoreType.DMA((6,)),
            pltpu.SemaphoreType.DMA((kinds, slabs)),
            pltpu.SemaphoreType.DMA((kinds, slabs)),
        ],
        compiler_params=pltpu.CompilerParams(
            collective_id=0, has_side_effects=True, vmem_limit_bytes=24 * 2**20
        ),
    )(
        initial_states.reshape(flat), coarse_decay.reshape(flat), power_map.reshape(flat),
        power_mask, region_ids, region_conductivity,
    )
    return states.reshape(initial_states.shape), jump.reshape(initial_states.shape)


def solution(mesh):
    return jax.shard_map(
        functools.partial(shards, mesh.shape["tm"]),
        mesh=mesh,
        in_specs=(
            P("tm", None, "sx", "sy"),
            P("tm", None, "sx", "sy"),
            P(None, "sx", "sy"),
            P("tm", None, None),
            P(),
            P(),
        ),
        out_specs=(P("tm", None, "sx", "sy"), P("tm", None, "sx", "sy")),
        check_vma=False,
    )
```

time: 633 us -> 49.5 us (0.08)
  waiting for transfers between devices: 433 us -> 0 us
  starting transfers between devices: 137 us -> 0 us
  Pallas kernels: 0 us -> 43.3 us
  other arithmetic: 36.1 us -> 0 us
  between operations: 15.8 us -> 0.66 us
    ppermute x97 -> x0, waiting for transfers between devices: 200 us -> none  [the longest x48 138 us: padded_2(): after = lax.ppermute(initial, axis, down)]
    psum x2 -> x0, waiting for transfers between devices: 139 us -> none  [broadcast(): return lax.psum(jnp.where(mine, x, jnp.zeros_like(x)), axis)]
    ppermute x97 -> x0, starting transfers between devices: 137 us -> none  [the longest x48 72.3 us: padded_2(): before = lax.ppermute(last, axis, up)]
    all_gather x3 -> x0, waiting for transfers between devices: 93.5 us -> none  [entering(): everything = jax.tree.map(lambda part: lax.all_gather(part, axis), x)]
    pallas_call x0 -> x1, Pallas kernels: none -> 43.3 us  [shards(): pl.pallas_call(functools.partial(kernel, slabs, solvers, chunk), out_shap...]
    select_n x18 -> x0, other arithmetic: 18.7 us -> none  [the longest x16 17.2 us: step(): return jax.tree.map(lambda a, b: jnp.where(reached, a, b), new, before)]
    div x22 -> x0, other arithmetic: 8.75 us -> none  [relax(): return (right_side + summed) / denominator]
  transfers between devices with their start and end apart: 102 -> 0, of which waited for: 75 -> 0; matrix products, arithmetic and copies ran while one was open for 1% -> 0% of each run, Pallas kernels for 0% -> 0%
where the time goes in v1:
time: 49.5 us; the launch traced here: 49.3 us
  Pallas kernels  43.3 us (87%)
  local copies, waits for them, and re-layouts  5.38 us (11%)
  between operations  0.66 us (1%)
    pallas_call x1, Pallas kernels, shards(): pl.pallas_call(functools.partial(kernel, slabs, solvers, chunk), out_shap...  43.3 us
    unnamed x14, local copies, waits for them, and re-layouts  5.38 us

profile of v1, /device:TPU:0, one launch (start us, length us, event | category | flops | bytes accessed | tf_op | source)
XLA Modules:
  0.0 49.3 jit_solution(4122543542172997940)
XLA Ops:
  0.6 0.0 copy-start.3
  0.6 0.0 copy-start.5
  0.7 0.7 %copy-done.3 = s32[8,8]{1,0:T(8,128)S(1)} copy-done((s32[8,8]{1,0:T(8,128)S(1)}, s32[8,8]{1,0:T(8,128)}, u32[]{:S(2)}) %copy-start.3) | copy-done | bytes 280
  1.3 0.0 copy-done.5
  1.3 0.0 copy-start
  1.3 0.9 %copy-done = f32[1,8,32,128]{3,2,1,0:T(8,128)S(1)} copy-done((f32[1,8,32,128]{3,2,1,0:T(8,128)S(1)}, f32[1,8,32,128]{3,2,1,0:T(8,128)}, u32[]{:S(2)}) %copy-start) | copy-done | bytes 131096
  2.2 0.0 copy-start.1
  2.2 0.9 %copy-done.1 = f32[1,8,32,128]{3,2,1,0:T(8,128)S(1)} copy-done((f32[1,8,32,128]{3,2,1,0:T(8,128)S(1)}, f32[1,8,32,128]{3,2,1,0:T(8,128)}, u32[]{:S(2)}) %copy-start.1) | copy-done | bytes 131096
  3.1 0.0 copy-start.2
  3.1 0.9 %copy-done.2 = f32[8,32,128]{2,1,0:T(8,128)S(1)} copy-done((f32[8,32,128]{2,1,0:T(8,128)S(1)}, f32[8,32,128]{2,1,0:T(8,128)}, u32[]{:S(2)}) %copy-start.2) | copy-done | bytes 131096
  4.0 0.0 copy-start.4
  4.0 0.7 %copy-done.4 = s32[1,4,8]{2,1,0:T(4,128)S(1)} copy-done((s32[1,4,8]{2,1,0:T(4,128)S(1)}, s32[1,4,8]{2,1,0:T(4,128)}, u32[]{:S(2)}) %copy-start.4) | copy-done | bytes 152
  4.7 43.3 %shard_map.77 = (f32[256,128]{1,0:T(8,128)S(1)}, f32[256,128]{1,0:T(8,128)S(1)}) custom-call(f32[256,128]{1,0:T(8,128)S(1)} %bitcast.5, f32[256,128]{1,0:T(8,128)S(1)} %bitcast.6, f32[256,128]{1,0:T(8,128)S(1)} %bitcast.7, s32[1,4,8]{2,1,0:T(4,128)S(1)} %copy-done.4, s32[8,8]{1,0:T(8,128)S(1)} %copy-done.3, f32[4]{0:T(128)S(1)} %copy-done.5), custom_call_target="tpu_custom_call" | custom-call | tf_op jit(solution)/shard_map/pallas_call | solution.py:355
  48.0 0.7 %copy.10 = f32[1,8,32,128]{3,2,1,0:T(8,128)} copy(f32[1,8,32,128]{3,2,1,0:T(8,128)S(1)} %bitcast.9) | data formatting | bytes 262144
  48.7 0.7 %copy.11 = f32[1,8,32,128]{3,2,1,0:T(8,128)} copy(f32[1,8,32,128]{3,2,1,0:T(8,128)S(1)} %bitcast.8) | data formatting | bytes 262144
Async XLA Ops:
  0.6 0.7 %copy-start.3 = (s32[8,8]{1,0:T(8,128)S(1)}, s32[8,8]{1,0:T(8,128)}, u32[]{:S(2)}) copy-start(s32[8,8]{1,0:T(8,128)} %ids_ref.1) | copy-start | bytes 772
  0.6 0.7 %copy-start.5 = (f32[4]{0:T(128)S(1)}, f32[4]{0:T(128)}, u32[]{:S(2)}) copy-start(f32[4]{0:T(128)} %cond_ref.1) | copy-start | bytes 52
  1.3 0.9 %copy-start = (f32[1,8,32,128]{3,2,1,0:T(8,128)S(1)}, f32[1,8,32,128]{3,2,1,0:T(8,128)}, u32[]{:S(2)}) copy-start(f32[1,8,32,128]{3,2,1,0:T(8,128)} %param.6) | copy-start | bytes 393220
  2.2 0.9 %copy-start.1 = (f32[1,8,32,128]{3,2,1,0:T(8,128)S(1)}, f32[1,8,32,128]{3,2,1,0:T(8,128)}, u32[]{:S(2)}) copy-start(f32[1,8,32,128]{3,2,1,0:T(8,128)} %param.7) | copy-start | bytes 393220
  3.1 0.9 %copy-start.2 = (f32[8,32,128]{2,1,0:T(8,128)S(1)}, f32[8,32,128]{2,1,0:T(8,128)}, u32[]{:S(2)}) copy-start(f32[8,32,128]{2,1,0:T(8,128)} %param.8) | copy-start | bytes 393220
  4.0 0.7 %copy-start.4 = (s32[1,4,8]{2,1,0:T(4,128)S(1)}, s32[1,4,8]{2,1,0:T(4,128)}, u32[]{:S(2)}) copy-start(s32[1,4,8]{2,1,0:T(4,128)} %mask_ref.1) | copy-start | bytes 388

commit v2 on v1

--- a/solution.py
+++ b/solution.py
@@ -16,7 +16,6 @@
 COLS = 128
 HALO = FSTEPS * SWEEPS
 EXT = ROWS + HALO
-PAD = 48
 STRIP = 16
 BLOCK = 4
 
@@ -27,8 +26,9 @@
 
 def kernel(
     slabs, solvers, chunk,
-    state_ref, decay_ref, power_ref, mask_ref, ids_ref, cond_ref,
+    state_hbm, decay_hbm, power_hbm, mask_hbm, ids_hbm, cond_hbm,
     out_ref, jump_ref,
+    state_ref, decay_ref, power_ref, mask_ref, ids_ref, cond_ref, load_sem,
     own, dec, off, packed, rows_in, side_in, corner_in,
     v, cond, rhs, wx, wy, wz, rden, power, base,
     a_in, b_in, u_out, u_in,
@@ -36,6 +36,16 @@
 ):
     tm, sx, sy = lax.axis_index("tm"), lax.axis_index("sx"), lax.axis_index("sy")
     other_core, side, corner = (tm, 1 - sx, sy), (tm, sx, 1 - sy), (tm, 1 - sx, 1 - sy)
+
+    loads = [
+        pltpu.make_async_copy(src, dst, load_sem.at[i])
+        for i, (src, dst) in enumerate((
+            (state_hbm, state_ref), (power_hbm, power_ref), (decay_hbm, decay_ref),
+            (ids_hbm, ids_ref), (cond_hbm, cond_ref), (mask_hbm, mask_ref),
+        ))
+    ]
+    for load in loads:
+        load.start()
 
     def slab_at(distance):
         return lax.rem(tm + distance, slabs)
@@ -72,6 +82,8 @@
         dec[r] = decay_ref[at, :]
         return carry
 
+    for load in loads:
+        load.wait()
     lax.fori_loop(0, ROWS, load_rows, 0, unroll=True)
     pack(None, 0)
     pack(None, 1)
@@ -99,22 +111,32 @@
         packed.at[pl.ds(0, 2), pl.ds(2, 2)], pl.ds(0, 2), 0,
     )
 
+    def chunk_of(t):
+        return t // 2 + (solvers // 2) * lax.rem(t + t // 2, 2)
+
+    def rows_of(t):
+        return pl.ds(chunk_of(t) * chunk, chunk)
+
     def to_solvers(src, dst, kind):
         def copy_at(d):
             target = slab_at(d)
             return pltpu.make_async_remote_copy(
-                src_ref=src.at[pl.ds(target * chunk, chunk)], dst_ref=dst.at[tm],
+                src_ref=src.at[rows_of(target)], dst_ref=dst.at[tm],
                 send_sem=far_send.at[kind, d], recv_sem=far_recv.at[kind, d],
                 device_id=(target, sx, sy), device_id_type=MESH,
             )
 
-        for d in range(1, slabs):
-            guarded(slab_at(d) < solvers, copy_at(d).start)
+        def send(half):
+            for d in range(1, slabs):
+                target = slab_at(d)
+                mine = chunk_of(target) // (solvers // 2) == half
+                pl.when(mine & (target < solvers))(copy_at(d).start)
 
         def keep():
-            dst[tm] = src[pl.ds(tm * chunk, chunk)]
-
-        guarded(tm < solvers, keep)
+            def store():
+                dst[tm] = src[rows_of(tm)]
+
+            guarded(tm < solvers, store)
 
         def sent():
             for d in range(1, slabs):
@@ -124,7 +146,7 @@
             for d in range(1, slabs):
                 copy_at(d).wait_recv()
 
-        return sent, arrived
+        return send, keep, sent, arrived
 
     def guarded(condition, action):
         if solvers == slabs:
@@ -132,19 +154,16 @@
         else:
             pl.when(condition)(action)
 
-    decay_sent, decay_arrived = to_solvers(dec, a_in, 0)
-
-    blank = jnp.zeros((BLOCK, LAYERS, 2 * COLS), jnp.float32)
-
-    def clear(i, carry):
-        at = pl.ds(BLOCK * i, BLOCK)
-        for slot in range(3):
-            v[slot, at] = blank
-        for ref in (cond, rhs, wx, wy, wz, rden, power):
-            ref[at] = blank
-        return carry
-
-    lax.fori_loop(0, PAD // BLOCK, clear, 0, unroll=True)
+    send, keep, decay_sent, decay_arrived = to_solvers(dec, a_in, 0)
+    send(0)
+    send(1)
+    keep()
+
+    blank = jnp.zeros((LAYERS, 2 * COLS), jnp.float32)
+    for stage in range(HALO + 1):
+        v[stage, 0] = blank
+    for m in range(FSTEPS):
+        cond[m, 0] = blank
 
     layer = lax.broadcasted_iota(jnp.int32, (LAYERS, 2 * COLS), 0)
     place = lax.broadcasted_iota(jnp.int32, (LAYERS, 2 * COLS), 1)
@@ -164,12 +183,15 @@
         + jnp.where(last_col, 1.0, 0.0)
     )
 
-    def spread(store, slot):
+    def spread_side(store, slot):
+        for i in range(8):
+            for g in range(ROWS // 8):
+                store(8 * g + i, 1, pltpu.roll(side_in[slot, g], (COLS - STRIP * i) % COLS, 1))
+
+    def spread_far(store, slot):
         for i in range(HALO):
             store(EXT - 1 - i, 0, rows_in[slot, i])
         for i in range(8):
-            for g in range(ROWS // 8):
-                store(8 * g + i, 1, pltpu.roll(side_in[slot, g], (COLS - STRIP * i) % COLS, 1))
             for g in range(2):
                 r = 2 * ROWS - 1 - (16 + 8 * g + i)
                 if r < EXT:
@@ -181,14 +203,26 @@
     def store_power(r, half, value):
         power[1 + r, :, half * COLS:(half + 1) * COLS] = value
 
-    def sweep(source, target, count, with_weights):
-        def body(i, carry):
-            r = BLOCK * i
-            at, before, after = pl.ds(r + 1, BLOCK), pl.ds(r, BLOCK), pl.ds(r + 2, BLOCK)
-            if with_weights:
-                k = cond[at]
-                west = k + cond[before]
-                east = k + cond[after]
+    def over(first, last, body):
+        full = (last - first) // BLOCK
+
+        def step(i, carry):
+            body(first + BLOCK * i, BLOCK)
+            return carry
+
+        lax.fori_loop(0, full, step, 0, unroll=True)
+        if first + BLOCK * full < last:
+            body(first + BLOCK * full, last - first - BLOCK * full)
+
+    def sweep(m, index, first, last):
+        source = SWEEPS * m + index
+
+        def body(r, size):
+            at, before, after = pl.ds(r + 1, size), pl.ds(r, size), pl.ds(r + 2, size)
+            if index == 0:
+                k = cond[m, at]
+                west = k + cond[m, before]
+                east = k + cond[m, after]
                 south = wy_mask * (k + pltpu.roll(k, 1, 2))
                 down = wz_mask * (k + pltpu.roll(k, 1, 1))
                 den = 1.0 + (
@@ -196,51 +230,54 @@
                     + down + pltpu.roll(down, LAYERS - 1, 1) + border * k
                 )
                 inverse = 1.0 / den
-                wx[at] = west
-                wy[at] = south
-                wz[at] = down
-                rden[at] = inverse
+                wx[m, at] = west
+                wy[m, at] = south
+                wz[m, at] = down
+                rden[m, at] = inverse
             else:
-                west, east, south, down, inverse = wx[at], wx[after], wy[at], wz[at], rden[at]
+                west, east, south = wx[m, at], wx[m, after], wy[m, at]
+                down, inverse = wz[m, at], rden[m, at]
             mid = v[source, at]
-            total = rhs[at] + west * v[source, before] + east * v[source, after]
+            total = rhs[m, at] + west * v[source, before] + east * v[source, after]
             total = total + south * pltpu.roll(mid, 1, 2)
             total = total + pltpu.roll(south * mid, 2 * COLS - 1, 2)
             total = total + down * pltpu.roll(mid, 1, 1)
             total = total + pltpu.roll(down * mid, LAYERS - 1, 1)
-            v[target, at] = total * inverse
-            return carry
-
-        lax.fori_loop(0, -(-count // BLOCK), body, 0, unroll=True)
-
-    def fine():
-        now, old, spare = 0, 1, 2
+            v[source + 1, at] = total * inverse
+
+        over(first, last, body)
+
+    def prepare(m, first, last):
+        coef_now, coef_old, scale = (1.0, 0.0, 1.0) if m == 0 else (4.0 / 3.0, -1.0 / 3.0, 2.0 / 3.0)
+        half = 0.5 * scale
+        now = SWEEPS * m
+
+        def body(r, size):
+            at = pl.ds(r + 1, size)
+            block = r // RB
+            current = v[now, at]
+            t = jnp.tanh(current)
+            cond[m, at] = base[block] * (half - (half * cond_slope) * t)
+            on = half * mask_ref[0, m, grid_block(block)].astype(jnp.float32)
+            total = (on * power[at]) * (1.0 + joule_slope * t)
+            if m == 0:
+                total = total + current
+            else:
+                total = total + (coef_now * current + coef_old * v[now - SWEEPS, at])
+            rhs[m, at] = total
+
+        aligned = min(-(-first // BLOCK) * BLOCK, last)
+        if first < aligned:
+            body(first, aligned - first)
+        over(aligned, last, body)
+
+    def fine(done, reached):
         for m in range(FSTEPS):
-            coef_now, coef_old, scale = (1.0, 0.0, 1.0) if m == 0 else (4.0 / 3.0, -1.0 / 3.0, 2.0 / 3.0)
-            half = 0.5 * scale
-            reach = EXT - SWEEPS * m
-
-            def prepare(i, carry, m=m, now=now, old=old, coef_now=coef_now, coef_old=coef_old, half=half):
-                at = pl.ds(BLOCK * i + 1, BLOCK)
-                block = (BLOCK * i) // RB
-                current = v[now, at]
-                t = jnp.tanh(current)
-                cond[at] = base[block] * (half - (half * cond_slope) * t)
-                on = half * mask_ref[0, m, grid_block(block)].astype(jnp.float32)
-                total = (on * power[at]) * (1.0 + joule_slope * t)
-                if m == 0:
-                    total = total + current
-                else:
-                    total = total + (coef_now * current + coef_old * v[old, at])
-                rhs[at] = total
-                return carry
-
-            lax.fori_loop(0, -(-reach // BLOCK), prepare, 0, unroll=True)
-            sweep(now, spare, reach - 1, True)
-            sweep(spare, old, reach - 2, False)
-            sweep(old, spare, reach - 3, False)
-            now, old, spare = spare, now, old
-        return now
+            left = SWEEPS * (FSTEPS - m)
+            prepare(m, done + left if done else 0, reached + left)
+            for index in range(SWEEPS):
+                left -= 1
+                sweep(m, index, done + left if done else 0, reached + left)
 
     def solve(it):
         a = [a_in[n] for n in range(slabs)]
@@ -261,7 +298,7 @@
         def copy_at(d):
             target = slab_at(d)
             return pltpu.make_async_remote_copy(
-                src_ref=u_out.at[it, target], dst_ref=u_in.at[it, pl.ds(tm * chunk, chunk)],
+                src_ref=u_out.at[it, target], dst_ref=u_in.at[it, rows_of(tm)],
                 send_sem=far_send.at[kind, d], recv_sem=far_recv.at[kind, d],
                 device_id=(target, sx, sy), device_id_type=MESH,
             )
@@ -270,7 +307,7 @@
             solve(it)
             for d in range(1, slabs):
                 copy_at(d).start()
-            u_in[it, pl.ds(tm * chunk, chunk)] = u_out[it, tm]
+            u_in[it, rows_of(tm)] = u_out[it, tm]
 
         guarded(tm < solvers, work)
 
@@ -288,43 +325,53 @@
     for r in range(ROWS):
         store_state(r, 0, own[0, r])
         store_power(r, 0, own[1, r])
-    for copy in first:
-        copy.wait_recv()
+    corner_copy, side_copy, rows_copy = first
     pending += [copy.wait_send for copy in first]
-    spread(store_state, 0)
-    spread(store_power, 1)
+    side_copy.wait_recv()
+    spread_side(store_state, 0)
+    spread_side(store_power, 1)
 
     for it in range(ITERS):
         if it:
-            for r in range(ROWS):
-                store_state(r, 0, u_in[it - 1, r])
             pack(it - 1, 0)
             again = near(
                 u_in.at[pl.ds(it - 1, 1), pl.ds(ROWS - HALO, HALO)], packed.at[pl.ds(2, 1)],
                 packed.at[pl.ds(2, 1), pl.ds(2, 2)], pl.ds(2, 1), 3,
             )
-            for copy in again:
-                copy.wait_recv()
+            corner_copy, side_copy, rows_copy = again
             pending += [copy.wait_send for copy in again]
-            spread(store_state, 2)
-        end = fine()
-
-        def offsets(i, carry, it=it, end=end):
-            at = pl.ds(BLOCK * i, BLOCK)
+            for r in range(ROWS):
+                store_state(r, 0, u_in[it - 1, r])
+            side_copy.wait_recv()
+            spread_side(store_state, 2)
+        send, keep, sent, arrived = to_solvers(off.at[it], b_in.at[it], 1 + it)
+
+        def offsets(r, size, it=it):
+            at = pl.ds(r, size)
             start = own[0, at] if it == 0 else u_in[it - 1, at]
-            off[it, at] = v[end, pl.ds(BLOCK * i + 1, BLOCK), :, 0:COLS] - dec[at] * start
-            return carry
-
-        lax.fori_loop(0, ROWS // BLOCK, offsets, 0, unroll=True)
-        sent, arrived = to_solvers(off.at[it], b_in.at[it], 1 + it)
+            off[it, at] = v[HALO, pl.ds(r + 1, size), :, 0:COLS] - dec[at] * start
+
+        middle = ROWS // 2
+        fine(0, middle)
+        over(0, middle, offsets)
+        send(0)
+        rows_copy.wait_recv()
+        corner_copy.wait_recv()
+        spread_far(store_state, 2 if it else 0)
+        if it == 0:
+            spread_far(store_power, 1)
+        fine(middle, ROWS)
+        over(middle, ROWS, offsets)
+        send(1)
+        keep()
         pending.append(sent)
         if it == 0:
             guarded(tm < solvers, decay_arrived)
         if it == ITERS - 1:
 
-            def jumps(r, carry, it=it, end=end):
+            def jumps(r, carry, it=it):
                 following = dec[r] * u_in[it - 1, r] + off[it - 1, r]
-                jump_ref[pl.ds(grid_row(r), LAYERS, ROWS), :] = v[end, r + 1, :, 0:COLS] - following
+                jump_ref[pl.ds(grid_row(r), LAYERS, ROWS), :] = v[HALO, r + 1, :, 0:COLS] - following
                 return carry
 
             lax.fori_loop(0, ROWS, jumps, 0, unroll=True)
@@ -348,16 +395,22 @@
     flat = (LAYERS * ROWS, COLS)
     f32 = jnp.float32
     tile = (ROWS, LAYERS, COLS)
-    wide = (PAD, LAYERS, 2 * COLS)
+    wide = (EXT + 2, LAYERS, 2 * COLS)
+    steps = (FSTEPS,) + wide
     vmem = pl.BlockSpec(memory_space=pltpu.VMEM)
-    smem = pl.BlockSpec(memory_space=pltpu.SMEM)
+    anywhere = pl.BlockSpec(memory_space=pl.ANY)
     kinds = 1 + 2 * ITERS
     states, jump = pl.pallas_call(
         functools.partial(kernel, slabs, solvers, chunk),
         out_shape=[jax.ShapeDtypeStruct(flat, f32)] * 2,
-        in_specs=[vmem] * 3 + [smem] * 3,
+        in_specs=[anywhere] * 6,
         out_specs=[vmem] * 2,
         scratch_shapes=[
+            *[pltpu.VMEM(flat, f32) for _ in range(3)],
+            pltpu.SMEM(power_mask.shape, jnp.int32),
+            pltpu.SMEM(region_ids.shape, jnp.int32),
+            pltpu.SMEM(region_conductivity.shape, f32),
+            pltpu.SemaphoreType.DMA((6,)),
             pltpu.VMEM((2,) + tile, f32),
             pltpu.VMEM(tile, f32),
             pltpu.VMEM((ITERS,) + tile, f32),
@@ -365,8 +418,9 @@
             pltpu.VMEM((3, HALO, LAYERS, COLS), f32),
             pltpu.VMEM((3, ROWS // 8, LAYERS, COLS), f32),
             pltpu.VMEM((3, 2, LAYERS, COLS), f32),
-            pltpu.VMEM((3,) + wide, f32),
-            *[pltpu.VMEM(wide, f32) for _ in range(7)],
+            pltpu.VMEM((HALO + 1,) + wide, f32),
+            *[pltpu.VMEM(steps, f32) for _ in range(6)],
+            pltpu.VMEM(wide, f32),
             pltpu.VMEM((-(-EXT // RB), LAYERS, 2 * COLS), f32),
             pltpu.VMEM((slabs, chunk, LAYERS, COLS), f32),
             pltpu.VMEM((ITERS, slabs, chunk, LAYERS, COLS), f32),
@@ -378,7 +432,7 @@
             pltpu.SemaphoreType.DMA((kinds, slabs)),
         ],
         compiler_params=pltpu.CompilerParams(
-            collective_id=0, has_side_effects=True, vmem_limit_bytes=24 * 2**20
+            collective_id=0, has_side_effects=True, vmem_limit_bytes=56 * 2**20
         ),
     )(
         initial_states.reshape(flat), coarse_decay.reshape(flat), power_map.reshape(flat),

time: 49.5 us -> 43.9 us (0.89)
  local copies, waits for them, and re-layouts: 5.38 us -> 2.26 us
  Pallas kernels: 43.3 us -> 40.8 us
    unnamed x14 -> x4, local copies, waits for them, and re-layouts: 5.38 us -> 2.26 us
    pallas_call x1, Pallas kernels: 43.3 us -> 40.8 us  [shards(): pl.pallas_call(functools.partial(kernel, slabs, solvers, chunk), out_shap...]
where the time goes in v2:
time: 43.9 us; the launch traced here: 43.7 us
  Pallas kernels  40.8 us (93%)
  local copies, waits for them, and re-layouts  2.26 us (5%)
  between operations  0.65 us (1%)
    pallas_call x1, Pallas kernels, shards(): pl.pallas_call(functools.partial(kernel, slabs, solvers, chunk), out_shap...  40.8 us
    unnamed x4, local copies, waits for them, and re-layouts  2.26 us

profile of v2, /device:TPU:0, one launch (start us, length us, event | category | flops | bytes accessed | tf_op | source)
XLA Modules:
  0.0 43.7 jit_solution(12666643248681494042)
XLA Ops:
  0.6 40.8 %shard_map.77 = (f32[256,128]{1,0:T(8,128)}, f32[256,128]{1,0:T(8,128)}) custom-call(f32[256,128]{1,0:T(8,128)} %bitcast.5, f32[256,128]{1,0:T(8,128)} %bitcast.6, f32[256,128]{1,0:T(8,128)} %bitcast.7, s32[1,4,8]{2,1,0:T(4,128)} %mask_hbm.1, s32[8,8]{1,0:T(8,128)} %ids_hbm.1, f32[4]{0:T(128)} %cond_hbm.1), custom_call_target="tpu_custom_call" | custom-call | tf_op jit(solution)/shard_map/pallas_call | solution.py:403
  41.4 0.0 copy-start
  41.5 1.6 %copy.10 = f32[1,8,32,128]{3,2,1,0:T(8,128)} copy(f32[1,8,32,128]{3,2,1,0:T(8,128)} %bitcast.9) | data formatting | bytes 262144
  43.1 0.0 copy-done
  43.1 0.7 %copy.11 = f32[1,8,32,128]{3,2,1,0:T(8,128)} copy(f32[1,8,32,128]{3,2,1,0:T(8,128)S(1)} %bitcast.8) | data formatting | bytes 262144
Async XLA Ops:
  41.4 1.6 %copy-start = (f32[256,128]{1,0:T(8,128)S(1)}, f32[256,128]{1,0:T(8,128)}, u32[]{:S(2)}) copy-start(f32[256,128]{1,0:T(8,128)} %get-tuple-element.5) | copy-start | bytes 393220

commit v3 on v2

--- a/solution.py
+++ b/solution.py
@@ -66,8 +66,8 @@
     window = lax.rem(lane // STRIP + 8, 8)
     edge_window = 7 * (1 - sy)
 
-    def pack(slot, kind):
-        for g in range(ROWS // 8):
+    def pack(slot, kind, first, last):
+        for g in range(first // 8, last // 8):
             total = own[kind, 8 * g] if slot is None else u_in[slot, 8 * g]
             for i in range(1, 8):
                 row = own[kind, 8 * g + i] if slot is None else u_in[slot, 8 * g + i]
@@ -85,8 +85,8 @@
     for load in loads:
         load.wait()
     lax.fori_loop(0, ROWS, load_rows, 0, unroll=True)
-    pack(None, 0)
-    pack(None, 1)
+    pack(None, 0, 0, ROWS)
+    pack(None, 1, 0, ROWS)
 
     pl.semaphore_wait(barrier, 3 + slabs - 1)
 
@@ -111,32 +111,27 @@
         packed.at[pl.ds(0, 2), pl.ds(2, 2)], pl.ds(0, 2), 0,
     )
 
-    def chunk_of(t):
-        return t // 2 + (solvers // 2) * lax.rem(t + t // 2, 2)
-
-    def rows_of(t):
-        return pl.ds(chunk_of(t) * chunk, chunk)
-
-    def to_solvers(src, dst, kind):
+    middle = ROWS // 2
+
+    def rows_of(half, t):
+        return pl.ds(half * middle + t * chunk, chunk)
+
+    def to_solvers(src, dst, kind, half):
         def copy_at(d):
             target = slab_at(d)
             return pltpu.make_async_remote_copy(
-                src_ref=src.at[rows_of(target)], dst_ref=dst.at[tm],
-                send_sem=far_send.at[kind, d], recv_sem=far_recv.at[kind, d],
+                src_ref=src.at[rows_of(half, target)], dst_ref=dst.at[half, tm],
+                send_sem=far_send.at[kind + half, d], recv_sem=far_recv.at[kind + half, d],
                 device_id=(target, sx, sy), device_id_type=MESH,
             )
 
-        def send(half):
-            for d in range(1, slabs):
-                target = slab_at(d)
-                mine = chunk_of(target) // (solvers // 2) == half
-                pl.when(mine & (target < solvers))(copy_at(d).start)
+        for d in range(1, slabs):
+            guarded(slab_at(d) < solvers, copy_at(d).start)
 
         def keep():
-            def store():
-                dst[tm] = src[rows_of(tm)]
-
-            guarded(tm < solvers, store)
+            dst[half, tm] = src[rows_of(half, tm)]
+
+        guarded(tm < solvers, keep)
 
         def sent():
             for d in range(1, slabs):
@@ -146,7 +141,8 @@
             for d in range(1, slabs):
                 copy_at(d).wait_recv()
 
-        return send, keep, sent, arrived
+        pending.append(sent)
+        return lambda: guarded(tm < solvers, arrived)
 
     def guarded(condition, action):
         if solvers == slabs:
@@ -154,10 +150,8 @@
         else:
             pl.when(condition)(action)
 
-    send, keep, decay_sent, decay_arrived = to_solvers(dec, a_in, 0)
-    send(0)
-    send(1)
-    keep()
+    pending = []
+    decay_arrived = [to_solvers(dec, a_in, 0, half) for half in range(2)]
 
     blank = jnp.zeros((LAYERS, 2 * COLS), jnp.float32)
     for stage in range(HALO + 1):
@@ -229,7 +223,8 @@
                     west + east + south + pltpu.roll(south, 2 * COLS - 1, 2)
                     + down + pltpu.roll(down, LAYERS - 1, 1) + border * k
                 )
-                inverse = 1.0 / den
+                guess = pl.reciprocal(den, approx=True)
+                inverse = guess * (2.0 - den * guess)
                 wx[m, at] = west
                 wy[m, at] = south
                 wz[m, at] = down
@@ -243,7 +238,11 @@
             total = total + pltpu.roll(south * mid, 2 * COLS - 1, 2)
             total = total + down * pltpu.roll(mid, 1, 1)
             total = total + pltpu.roll(down * mid, LAYERS - 1, 1)
-            v[source + 1, at] = total * inverse
+            total = total * inverse
+            if source + 1 < HALO:
+                v[source + 1, at] = total
+            else:
+                v[source + 1, at, :, 0:COLS] = total[:, :, 0:COLS]
 
         over(first, last, body)
 
@@ -279,35 +278,35 @@
                 left -= 1
                 sweep(m, index, done + left if done else 0, reached + left)
 
-    def solve(it):
-        a = [a_in[n] for n in range(slabs)]
-        total = b_in[it, 0]
+    def solve(it, half):
+        a = [a_in[half, n] for n in range(slabs)]
+        total = b_in[it, half, 0]
         product = a[0]
         for n in range(1, slabs):
-            total = a[n] * total + b_in[it, n]
+            total = a[n] * total + b_in[it, half, n]
             product = product * a[n]
         state = total / (1.0 - product)
         for n in range(slabs):
-            u_out[it, n] = state
+            u_out[it, half, n] = state
             if n < slabs - 1:
-                state = a[n] * state + b_in[it, n]
-
-    def from_solvers(it):
-        kind = 1 + ITERS + it
+                state = a[n] * state + b_in[it, half, n]
+
+    def from_solvers(it, half):
+        kind = 2 + 2 * (ITERS + it) + half
 
         def copy_at(d):
             target = slab_at(d)
             return pltpu.make_async_remote_copy(
-                src_ref=u_out.at[it, target], dst_ref=u_in.at[it, rows_of(tm)],
+                src_ref=u_out.at[it, half, target], dst_ref=u_in.at[it, rows_of(half, tm)],
                 send_sem=far_send.at[kind, d], recv_sem=far_recv.at[kind, d],
                 device_id=(target, sx, sy), device_id_type=MESH,
             )
 
         def work():
-            solve(it)
+            solve(it, half)
             for d in range(1, slabs):
                 copy_at(d).start()
-            u_in[it, rows_of(tm)] = u_out[it, tm]
+            u_in[it, rows_of(half, tm)] = u_out[it, half, tm]
 
         guarded(tm < solvers, work)
 
@@ -319,9 +318,9 @@
             for d in range(1, slabs):
                 guarded(lax.rem(tm - d + slabs, slabs) < solvers, copy_at(d).wait_recv)
 
-        return lambda: guarded(tm < solvers, sent), arrived
-
-    pending = [decay_sent]
+        pending.append(lambda: guarded(tm < solvers, sent))
+        return arrived
+
     for r in range(ROWS):
         store_state(r, 0, own[0, r])
         store_power(r, 0, own[1, r])
@@ -333,28 +332,28 @@
 
     for it in range(ITERS):
         if it:
-            pack(it - 1, 0)
+            for half in range(2):
+                arrived[half]()
+                for r in range(half * middle, (half + 1) * middle):
+                    store_state(r, 0, u_in[it - 1, r])
+                pack(it - 1, 0, half * middle, (half + 1) * middle)
             again = near(
                 u_in.at[pl.ds(it - 1, 1), pl.ds(ROWS - HALO, HALO)], packed.at[pl.ds(2, 1)],
                 packed.at[pl.ds(2, 1), pl.ds(2, 2)], pl.ds(2, 1), 3,
             )
             corner_copy, side_copy, rows_copy = again
             pending += [copy.wait_send for copy in again]
-            for r in range(ROWS):
-                store_state(r, 0, u_in[it - 1, r])
             side_copy.wait_recv()
             spread_side(store_state, 2)
-        send, keep, sent, arrived = to_solvers(off.at[it], b_in.at[it], 1 + it)
 
         def offsets(r, size, it=it):
             at = pl.ds(r, size)
             start = own[0, at] if it == 0 else u_in[it - 1, at]
             off[it, at] = v[HALO, pl.ds(r + 1, size), :, 0:COLS] - dec[at] * start
 
-        middle = ROWS // 2
         fine(0, middle)
         over(0, middle, offsets)
-        send(0)
+        lower = to_solvers(off.at[it], b_in.at[it], 2 + 2 * it, 0)
         rows_copy.wait_recv()
         corner_copy.wait_recv()
         spread_far(store_state, 2 if it else 0)
@@ -362,11 +361,12 @@
             spread_far(store_power, 1)
         fine(middle, ROWS)
         over(middle, ROWS, offsets)
-        send(1)
-        keep()
-        pending.append(sent)
+        upper = to_solvers(off.at[it], b_in.at[it], 2 + 2 * it, 1)
         if it == 0:
-            guarded(tm < solvers, decay_arrived)
+            for wait in decay_arrived:
+                wait()
+        lower()
+        arrived = [from_solvers(it, 0)]
         if it == ITERS - 1:
 
             def jumps(r, carry, it=it):
@@ -375,23 +375,23 @@
                 return carry
 
             lax.fori_loop(0, ROWS, jumps, 0, unroll=True)
-        guarded(tm < solvers, arrived)
-        sent, arrived = from_solvers(it)
-        pending.append(sent)
-        arrived()
+        upper()
+        arrived.append(from_solvers(it, 1))
 
     def finish(r, carry):
         out_ref[pl.ds(grid_row(r), LAYERS, ROWS), :] = u_in[ITERS - 1, r]
         return carry
 
-    lax.fori_loop(0, ROWS, finish, 0, unroll=True)
+    for half in range(2):
+        arrived[half]()
+        lax.fori_loop(half * middle, (half + 1) * middle, finish, 0, unroll=True)
     for wait in pending:
         wait()
 
 
 def shards(slabs, initial_states, coarse_decay, power_map, power_mask, region_ids, region_conductivity):
-    solvers = min(slabs, ROWS)
-    chunk = ROWS // solvers
+    solvers = min(slabs, ROWS // 2)
+    chunk = ROWS // 2 // solvers
     flat = (LAYERS * ROWS, COLS)
     f32 = jnp.float32
     tile = (ROWS, LAYERS, COLS)
@@ -399,7 +399,7 @@
     steps = (FSTEPS,) + wide
     vmem = pl.BlockSpec(memory_space=pltpu.VMEM)
     anywhere = pl.BlockSpec(memory_space=pl.ANY)
-    kinds = 1 + 2 * ITERS
+    kinds = 2 + 4 * ITERS
     states, jump = pl.pallas_call(
         functools.partial(kernel, slabs, solvers, chunk),
         out_shape=[jax.ShapeDtypeStruct(flat, f32)] * 2,
@@ -422,9 +422,9 @@
             *[pltpu.VMEM(steps, f32) for _ in range(6)],
             pltpu.VMEM(wide, f32),
             pltpu.VMEM((-(-EXT // RB), LAYERS, 2 * COLS), f32),
-            pltpu.VMEM((slabs, chunk, LAYERS, COLS), f32),
-            pltpu.VMEM((ITERS, slabs, chunk, LAYERS, COLS), f32),
-            pltpu.VMEM((ITERS, slabs, chunk, LAYERS, COLS), f32),
+            pltpu.VMEM((2, slabs, chunk, LAYERS, COLS), f32),
+            pltpu.VMEM((ITERS, 2, slabs, chunk, LAYERS, COLS), f32),
+            pltpu.VMEM((ITERS, 2, slabs, chunk, LAYERS, COLS), f32),
             pltpu.VMEM((ITERS,) + tile, f32),
             pltpu.SemaphoreType.DMA((6,)),
             pltpu.SemaphoreType.DMA((6,)),

time: 43.9 us -> 45.1 us (1.027)
  Pallas kernels: 40.8 us -> 42.1 us
    pallas_call x1, Pallas kernels: 40.8 us -> 42.1 us  [shards(): pl.pallas_call(functools.partial(kernel, slabs, solvers, chunk), out_shap...]
where the time goes in v3:
time: 45.1 us; the launch traced here: 45 us
  Pallas kernels  42.1 us (93%)
  local copies, waits for them, and re-layouts  2.26 us (5%)
  between operations  0.65 us (1%)
    pallas_call x1, Pallas kernels, shards(): pl.pallas_call(functools.partial(kernel, slabs, solvers, chunk), out_shap...  42.1 us
    unnamed x4, local copies, waits for them, and re-layouts  2.26 us

profile of v3, /device:TPU:0, one launch (start us, length us, event | category | flops | bytes accessed | tf_op | source)
XLA Modules:
  0.0 45.0 jit_solution(16967276608097906073)
XLA Ops:
  0.6 42.1 %shard_map.77 = (f32[256,128]{1,0:T(8,128)}, f32[256,128]{1,0:T(8,128)}) custom-call(f32[256,128]{1,0:T(8,128)} %bitcast.5, f32[256,128]{1,0:T(8,128)} %bitcast.6, f32[256,128]{1,0:T(8,128)} %bitcast.7, s32[1,4,8]{2,1,0:T(4,128)} %mask_hbm.1, s32[8,8]{1,0:T(8,128)} %ids_hbm.1, f32[4]{0:T(128)} %cond_hbm.1), custom_call_target="tpu_custom_call" | custom-call | tf_op jit(solution)/shard_map/pallas_call | solution.py:403
  42.7 0.0 copy-start
  42.7 1.6 %copy.10 = f32[1,8,32,128]{3,2,1,0:T(8,128)} copy(f32[1,8,32,128]{3,2,1,0:T(8,128)} %bitcast.9) | data formatting | bytes 262144
  44.3 0.0 copy-done
  44.3 0.7 %copy.11 = f32[1,8,32,128]{3,2,1,0:T(8,128)} copy(f32[1,8,32,128]{3,2,1,0:T(8,128)S(1)} %bitcast.8) | data formatting | bytes 262144
Async XLA Ops:
  42.7 1.6 %copy-start = (f32[256,128]{1,0:T(8,128)S(1)}, f32[256,128]{1,0:T(8,128)}, u32[]{:S(2)}) copy-start(f32[256,128]{1,0:T(8,128)} %get-tuple-element.5) | copy-start | bytes 393220

commit v4 on v2

--- a/solution.py
+++ b/solution.py
@@ -229,7 +229,8 @@
                     west + east + south + pltpu.roll(south, 2 * COLS - 1, 2)
                     + down + pltpu.roll(down, LAYERS - 1, 1) + border * k
                 )
-                inverse = 1.0 / den
+                guess = pl.reciprocal(den, approx=True)
+                inverse = guess * (2.0 - den * guess)
                 wx[m, at] = west
                 wy[m, at] = south
                 wz[m, at] = down
@@ -243,7 +244,11 @@
             total = total + pltpu.roll(south * mid, 2 * COLS - 1, 2)
             total = total + down * pltpu.roll(mid, 1, 1)
             total = total + pltpu.roll(down * mid, LAYERS - 1, 1)
-            v[source + 1, at] = total * inverse
+            total = total * inverse
+            if source + 1 < HALO:
+                v[source + 1, at] = total
+            else:
+                v[source + 1, at, :, 0:COLS] = total[:, :, 0:COLS]
 
         over(first, last, body)
 

time: 43.9 us -> 44 us (level)
  no operation moved by 1% of the time
where the time goes in v4:
time: 44 us; the launch traced here: 43.9 us
  Pallas kernels  41 us (93%)
  local copies, waits for them, and re-layouts  2.26 us (5%)
  between operations  0.65 us (1%)
    pallas_call x1, Pallas kernels, shards(): pl.pallas_call(functools.partial(kernel, slabs, solvers, chunk), out_shap...  41 us
    unnamed x4, local copies, waits for them, and re-layouts  2.26 us

profile of v4, /device:TPU:0, one launch (start us, length us, event | category | flops | bytes accessed | tf_op | source)
XLA Modules:
  0.0 43.9 jit_solution(5364222650878688885)
XLA Ops:
  0.6 41.0 %shard_map.77 = (f32[256,128]{1,0:T(8,128)}, f32[256,128]{1,0:T(8,128)}) custom-call(f32[256,128]{1,0:T(8,128)} %bitcast.5, f32[256,128]{1,0:T(8,128)} %bitcast.6, f32[256,128]{1,0:T(8,128)} %bitcast.7, s32[1,4,8]{2,1,0:T(4,128)} %mask_hbm.1, s32[8,8]{1,0:T(8,128)} %ids_hbm.1, f32[4]{0:T(128)} %cond_hbm.1), custom_call_target="tpu_custom_call" | custom-call | tf_op jit(solution)/shard_map/pallas_call | solution.py:408
  41.6 0.0 copy-start
  41.6 1.6 %copy.10 = f32[1,8,32,128]{3,2,1,0:T(8,128)} copy(f32[1,8,32,128]{3,2,1,0:T(8,128)} %bitcast.9) | data formatting | bytes 262144
  43.2 0.0 copy-done
  43.2 0.7 %copy.11 = f32[1,8,32,128]{3,2,1,0:T(8,128)} copy(f32[1,8,32,128]{3,2,1,0:T(8,128)S(1)} %bitcast.8) | data formatting | bytes 262144
Async XLA Ops:
  41.6 1.6 %copy-start = (f32[256,128]{1,0:T(8,128)S(1)}, f32[256,128]{1,0:T(8,128)}, u32[]{:S(2)}) copy-start(f32[256,128]{1,0:T(8,128)} %get-tuple-element.5) | copy-start | bytes 393220
